TPU v7x, 32 devices: a whole 2x2x4 slice. The times are simulated.
32 devices in a mesh: groups: 2 (over x), req: 16 (over z, y, core).
Axes of the slice: x: 2, y: 2, z: 4, core: 2. Of those that a mesh axis runs over, the one named last changes fastest.
Arguments:
- frames: bfloat16 [8192, 1280], P(('groups', 'req')), parts along dimension 0, may hold values from -6 to 6
- ln1_gain: bfloat16 [1280], replicated, may hold values from 0.5 to 1.5
- ln1_bias: bfloat16 [1280], replicated, may hold values from -3 to 3
- w_qkv: bfloat16 [2560, 3840], P('req'), may hold values from -1 to 1
- w_out: bfloat16 [2560, 1280], P('req'), may hold values from -0.15625 to 0.15625
- ln2_gain: bfloat16 [1280], replicated, may hold values from 0.5 to 1.5
- ln2_bias: bfloat16 [1280], replicated, may hold values from -3 to 3
- w_proj: bfloat16 [2560, 4096], P('req'), may hold values from -1 to 1, as said below
- b_proj: bfloat16 [4096], replicated, may hold values from -3 to 3
- text_embed: bfloat16 [8192, 4096], P(('groups', 'req')), parts along dimension 0, may hold values from -6 to 6
- rms_gain: bfloat16 [4096], replicated, may hold values from 0.5 to 1.5
- window_pairs: int32 [32, 4], P(('groups', 'req')), parts along dimension 0, may hold values from 1 to 64, 128 in all within a row
- row_route: int32 [4096, 1], P('groups'), parts along dimension 0, may hold values from 0 to 15; in each aligned block of 128 rows (0 to 127, 128 to 255, ...) at most 16 rows name the same one
Outputs:
- prefill_input: bfloat16 [16384, 4096], P(('groups', 'req')), parts along dimension 0
There are 2 independent parts, one for each index of `groups`. A program takes and returns all parts, laid end to end along the dimension named above; an argument that names none is the same for every part. Nothing has to cross between parts.
Inputs may be any that keep to these rules, and one draw needn't show every extreme that they name: `w_proj`: its 2 blocks of 1280 rows are equal. `window_pairs`: row j of device s gives the frame pairs of the j-th window of its queue; each row sums to 128. `row_route`: the pooled rows of one device name each prefill device at most 16 times.
All inputs are finite; a program needn't handle non-finite values.
Results may differ from a plain program's by a relative error of at most 0.0047.
Values may be sent and summed in bfloat16 or wider, within the bound.
A program may use at most 128 MiB of HBM per device.

v0:
```python
import jax
import jax.numpy as jnp
from jax import lax
from jax.sharding import PartitionSpec as P

HEAD = 64


def swapped(value, axis, distance):
    mask = 2**distance
    pairs = [(source, source ^ mask) for source in range(lax.axis_size(axis))]
    return lax.ppermute(value, axis, pairs)


def layer_norm(values_in, gain_row, bias_row, epsilon):
    row_mean = jnp.mean(values_in, axis=-1, keepdims=True)
    centered = values_in - row_mean
    variance = jnp.mean(centered * centered, axis=-1, keepdims=True)
    return centered * lax.rsqrt(variance + epsilon) * gain_row.astype(
        jnp.float32
    ) + bias_row.astype(jnp.float32)


def rms_rows(packed_rows, rms_gain):
    values_f32 = packed_rows.astype(jnp.float32)
    mean_square = jnp.mean(values_f32 * values_f32, axis=-1, keepdims=True)
    return (values_f32 * lax.rsqrt(mean_square + 1e-06) * rms_gain.astype(jnp.float32)).astype(
        jnp.bfloat16
    )


def window_ids(pair_counts, frame_count):
    window_ends = jnp.cumsum(pair_counts) * 2
    frame_index = jnp.arange(frame_count, dtype=jnp.int32)
    return jnp.sum((frame_index[:, None] >= window_ends[None, :]).astype(jnp.int32), axis=1)


def join_pair(mine, partner, upper):
    return jnp.where(
        upper, jnp.concatenate([partner, mine], axis=0), jnp.concatenate([mine, partner], axis=0)
    )


def attend(queries, key_rows, value_rows, window):
    score_scale = queries.shape[2] ** (-0.5)
    scores = (
        jnp.einsum("qhd,khd->hqk", queries, key_rows, preferred_element_type=jnp.float32)
        * score_scale
    )
    same_window = window[:, None] == window[None, :]
    scores = jnp.where(same_window[None], scores, -1e30)
    top_score = jnp.max(scores, axis=2, keepdims=True)
    expo_scores = jnp.exp(scores - top_score)
    weights = (expo_scores / jnp.sum(expo_scores, axis=2, keepdims=True)).astype(jnp.bfloat16)
    pieces = jnp.einsum(
        "hqk,khd->qhd", weights, value_rows, preferred_element_type=jnp.float32
    ).astype(jnp.bfloat16)
    return pieces


def project_audio(normed, w_proj, b_proj, my_index):
    whole_proj = w_proj
    for level in range(3):
        partner = swapped(whole_proj, "req", level)
        whole_proj = join_pair(whole_proj, partner, my_index >> level & 1 == 1)
    running = jnp.dot(normed, whole_proj, preferred_element_type=jnp.float32)
    return (running + b_proj.astype(jnp.float32)).astype(jnp.bfloat16)


def send_rows(buffer, devices):
    shaped = buffer.reshape(devices, buffer.shape[0] // devices, buffer.shape[1])
    arrived = lax.all_to_all(shaped, "req", split_axis=0, concat_axis=0, tiled=True)
    return arrived.reshape(buffer.shape[0], buffer.shape[1])


def body(
    frames,
    ln1_gain,
    ln1_bias,
    w_qkv,
    w_out,
    ln2_gain,
    ln2_bias,
    w_proj,
    b_proj,
    text_embed,
    rms_gain,
    window_pairs,
    row_route,
):
    frame_count = frames.shape[0]
    enc_width = frames.shape[1]
    devices = lax.axis_size("req")
    my_index = lax.axis_index("req")
    pooled_rows = frame_count // 2
    capacity = 2 * pooled_rows // devices
    text_normed = rms_rows(text_embed, rms_gain)
    frames_f32 = frames.astype(jnp.float32)
    normed_in = layer_norm(frames_f32, ln1_gain, ln1_bias, 1e-05).astype(jnp.bfloat16)
    whole_qkv = w_qkv
    for level in range(3):
        partner = swapped(whole_qkv, "req", level)
        whole_qkv = join_pair(whole_qkv, partner, my_index >> level & 1 == 1)
    whole_out = w_out
    for level in range(3):
        partner = swapped(whole_out, "req", level)
        whole_out = join_pair(whole_out, partner, my_index >> level & 1 == 1)
    qkv_proj = jnp.dot(normed_in, whole_qkv, preferred_element_type=jnp.float32)
    head_count = enc_width // HEAD
    queries = qkv_proj[:, :enc_width].astype(jnp.bfloat16).reshape(frame_count, head_count, HEAD)
    key_rows = (
        qkv_proj[:, enc_width : 2 * enc_width]
        .astype(jnp.bfloat16)
        .reshape(frame_count, head_count, HEAD)
    )
    value_rows = (
        qkv_proj[:, 2 * enc_width :].astype(jnp.bfloat16).reshape(frame_count, head_count, HEAD)
    )
    window = window_ids(window_pairs[0], frame_count)
    attended = attend(queries, key_rows, value_rows, window).reshape(frame_count, enc_width)
    mixed = jnp.dot(attended, whole_out, preferred_element_type=jnp.float32)
    encoded = frames_f32 + mixed
    pooled = (encoded[0::2] + encoded[1::2]) * 0.5
    normed = layer_norm(pooled, ln2_gain, ln2_bias, 1e-05).astype(jnp.bfloat16)
    route_table = row_route[:, 0].reshape(devices, pooled_rows)
    own_dest = lax.dynamic_index_in_dim(route_table, my_index, 0, keepdims=False)
    one_hot = (own_dest[:, None] == jnp.arange(devices, dtype=jnp.int32)[None, :]).astype(jnp.int32)
    slot_index = jnp.sum((jnp.cumsum(one_hot, axis=0) - one_hot) * one_hot, axis=1)
    target = own_dest * capacity + slot_index
    picker = (jnp.arange(devices * capacity, dtype=jnp.int32)[:, None] == target[None, :]).astype(
        jnp.bfloat16
    )
    embedded = project_audio(normed, w_proj, b_proj, my_index)
    buffer = jnp.dot(picker, embedded, preferred_element_type=jnp.float32).astype(jnp.bfloat16)
    arrived = send_rows(buffer, devices)
    audio_normed = rms_rows(arrived, rms_gain)
    return jnp.concatenate([audio_normed, text_normed], axis=0)


def solution(mesh):
    in_specs = (
        P(("groups", "req"), None),
        P(),
        P(),
        P("req", None),
        P("req", None),
        P(),
        P(),
        P("req", None),
        P(),
        P(("groups", "req"), None),
        P(),
        P(("groups", "req"), None),
        P("groups", None),
    )
    out_specs = P(("groups", "req"), None)
    return jax.shard_map(body, mesh=mesh, in_specs=in_specs, out_specs=out_specs, check_vma=False)
```

profile of v0, /device:TPU:0, one launch (start us, length us, event | category | flops | bytes accessed | tf_op | source)
XLA Modules:
  0.0 393.6 jit_solution(14837621983445762768)
XLA Ops:
  0.5 2.9 collective-permute-done
  3.3 2.7 maximum_select_fusion.17
  6.0 3.0 collective-permute-start.1
  9.0 53.8 %collective-permute-done.1 = bf16[320,3840]{1,0:T(8,128)(2,1)} collective-permute-done((bf16[320,3840]{1,0:T(8,128)(2,1)S(1)}, bf16[320,3840]{1,0:T(8,128)(2,1)}, u32[]{:S(2)}, u32[]{:S(2)}) %collective-permute-start.1) | collective-permute-done | bytes 2457632 | tf_op jit(solution)/shard_map/ppermute | solution.py:12
  62.7 6.2 %maximum_select_fusion.7 = bf16[640,3840]{1,0:T(8,128)(2,1)} fusion(bf16[320,3840]{1,0:T(8,128)(2,1)S(1)} %maximum_select_fusion.17, bf16[320,3840]{1,0:T(8,128)(2,1)} %collective-permute-done.1, pred[]{:T(512)S(6)} %eq.71), kind=kLoop, calls=%fused_computation.25 | loop fusion | flops 22118400 | bytes 9830401 | tf_op jit(solution)/shard_map/jit(_where)/select_n | solution.py:39
  68.9 1.9 collective-permute-start.2
  70.8 3.2 maximum_select_fusion.16
  74.0 1.6 collective-permute-start.7
  80.1 53.9 %collective-permute-done.7 = bf16[320,4096]{1,0:T(8,128)(2,1)} collective-permute-done((bf16[320,4096]{1,0:T(8,128)(2,1)S(1)}, bf16[320,4096]{1,0:T(8,128)(2,1)}, u32[]{:S(2)}, u32[]{:S(2)}) %collective-permute-start.7) | collective-permute-done | bytes 2621472 | tf_op jit(solution)/shard_map/ppermute | solution.py:12
  133.9 6.8 %maximum_select_fusion.4 = bf16[640,4096]{1,0:T(8,128)(2,1)} fusion(bf16[320,4096]{1,0:T(8,128)(2,1)S(1)} %maximum_select_fusion.16, bf16[320,4096]{1,0:T(8,128)(2,1)} %collective-permute-done.7, pred[]{:T(512)S(6)} %eq.71), kind=kLoop, calls=%fused_computation.19 | loop fusion | flops 23592960 | bytes 10485761 | tf_op jit(solution)/shard_map/jit(_where)/select_n | solution.py:39
  141.5 7.9 %collective-permute-done.4 = bf16[320,1280]{1,0:T(8,128)(2,1)S(1)} collective-permute-done((bf16[320,1280]{1,0:T(8,128)(2,1)S(1)}, bf16[320,1280]{1,0:T(8,128)(2,1)S(1)}, u32[]{:S(2)}, u32[]{:S(2)}) %collective-permute-start.4) | collective-permute-done | bytes 819232 | tf_op jit(solution)/shard_map/ppermute | solution.py:12
  149.4 1.8 maximum_select_fusion.18
  151.7 26.5 %collective-permute-done.2 = bf16[640,3840]{1,0:T(8,128)(2,1)} collective-permute-done((bf16[640,3840]{1,0:T(8,128)(2,1)}, bf16[640,3840]{1,0:T(8,128)(2,1)}, u32[]{:S(2)}, u32[]{:S(2)}) %collective-permute-start.2) | collective-permute-done | bytes 4915232 | tf_op jit(solution)/shard_map/ppermute | solution.py:12
  178.3 8.6 %fusion.15 = bf16[256,3840]{1,0:T(8,128)(2,1)S(1)} fusion(bf16[640,3840]{1,0:T(8,128)(2,1)} %maximum_select_fusion.7, bf16[640,3840]{1,0:T(8,128)(2,1)} %collective-permute-done.2, pred[]{:T(512)S(6)} %eq.70, bf16[256,1280]{1,0:T(8,128)(2,1)S(1)} %copy-done, f32[1280]{0:T(1024)S(1)} %convert_element_type.74, f32[1280]{0:T(1024)S(1)} %convert_element_type.73, ...), kind=kOutput, calls=%fused_computation.23 | convolution fusion | flops 2563768320 | bytes 12464129 | tf_op jit(solution)/shard_map/dot_general | solution.py:108
  187.8 4.2 %fusion.66 = (f32[20,256]{1,0:T(8,128)S(1)}, f32[20,256,256]{1,2,0:T(8,128)}) fusion(pred[256,256]{0,1:T(8,128)(4,1)S(1)} %broadcast_compare_fusion, bf16[256,20,64]{0,2,1:T(8,128)(2,1)S(1)} %bitcast.32, bf16[256,20,64]{0,2,1:T(8,128)(2,1)S(1)} %bitcast.33), kind=kOutput, calls=%fused_computation.101 | convolution fusion | flops 173015296 | bytes 6639616 | tf_op jit(solution)/shard_map/sub | solution.py:53
  192.0 3.1 fusion.38
  195.1 129.2 %collective-permute-done.5 = bf16[640,1280]{1,0:T(8,128)(2,1)} collective-permute-done((bf16[640,1280]{1,0:T(8,128)(2,1)}, bf16[640,1280]{1,0:T(8,128)(2,1)}, u32[]{:S(2)}, u32[]{:S(2)}) %collective-permute-start.5) | collective-permute-done | bytes 1638432 | tf_op jit(solution)/shard_map/ppermute | solution.py:12
  324.3 3.9 fusion.31
  329.9 10.3 %convolution_convert_fusion = bf16[256,4096]{1,0:T(8,128)(2,1)} fusion(bf16[640,4096]{1,0:T(8,128)(2,1)} %maximum_select_fusion.4, bf16[640,4096]{1,0:T(8,128)(2,1)} %collective-permute-done.8, pred[]{:T(512)S(6)} %eq.70, f32[4096]{0:T(1024)S(1)} %convert_element_type.83, f32[1280]{0:T(1024)S(1)} %convert_element_type.81, ...), kind=kOutput, calls=%fused_computation.24 | convolution fusion | flops 1661075456 | bytes 13921793 | tf_op jit(solution)/shard_map/dot_general | solution.py:134
  340.2 6.0 %all-to-all-start = ((bf16[16,16,4096]{2,1,0:T(8,128)(2,1)}), bf16[16,16,4096]{2,1,0:T(8,128)(2,1)S(1)}, u32[]{:S(2)}, u32[]{:S(2)}) async-start(bf16[16,16,4096]{2,1,0:T(8,128)(2,1)} %bitcast.31), calls=%async_computation | async-start | bytes 4194304 | tf_op jit(solution)/shard_map/all_to_all | solution.py:72
  346.2 2.1 fusion.18
  348.3 39.0 %all-to-all-done = bf16[16,16,4096]{2,1,0:T(8,128)(2,1)S(1)} async-done(((bf16[16,16,4096]{2,1,0:T(8,128)(2,1)}), bf16[16,16,4096]{2,1,0:T(8,128)(2,1)S(1)}, u32[]{:S(2)}, u32[]{:S(2)}) %all-to-all-start) | async-done | bytes 2097184 | tf_op jit(solution)/shard_map/all_to_all | solution.py:72
  387.8 3.2 fusion.22
  391.0 2.5 pad_maximum_fusion
  (59 shorter events, 9.1 us)
Async XLA Ops:
  0.0 3.3 collective-permute-start
  6.0 56.7 %collective-permute-start.1 = (bf16[320,3840]{1,0:T(8,128)(2,1)S(1)}, bf16[320,3840]{1,0:T(8,128)(2,1)}, u32[]{:S(2)}, u32[]{:S(2)}) collective-permute-start(bf16[320,3840]{1,0:T(8,128)(2,1)S(1)} %maximum_select_fusion.17), channel_id=1, source_target_pairs={{0,2},{1,3},{2,0},{3,1},{4,6},{5,7},{6,4},{7,5},{8,10},{9,11},{10,... | collective-permute-start | bytes 7372808 | tf_op jit(solution)/shard_map/ppermute | solution.py:12
  9.0 61.8 %collective-permute-start.6 = (bf16[160,4096]{1,0:T(8,128)(2,1)}, bf16[160,4096]{1,0:T(8,128)(2,1)}, u32[]{:S(2)}, u32[]{:S(2)}) collective-permute-start(bf16[160,4096]{1,0:T(8,128)(2,1)} %param.20), channel_id=1, source_target_pairs={{0,1},{1,0},{2,3},{3,2},{4,5},{5,4},{6,7},{7,6},{8,9},{9,8},{10,11... | collective-permute-start | bytes 3932168 | tf_op jit(solution)/shard_map/ppermute | solution.py:12
  68.9 6.7 %copy-start.3 = (bf16[1280]{0:T(1024)(128)(2,1)S(1)}, bf16[1280]{0:T(1024)(128)(2,1)}, u32[]{:S(2)}) copy-start(bf16[1280]{0:T(1024)(128)(2,1)} %param.14) | copy-start | bytes 7684
  68.9 6.7 %copy-start.4 = (bf16[1280]{0:T(1024)(128)(2,1)S(1)}, bf16[1280]{0:T(1024)(128)(2,1)}, u32[]{:S(2)}) copy-start(bf16[1280]{0:T(1024)(128)(2,1)} %param.15) | copy-start | bytes 7684
  68.9 6.7 %copy-start.7 = (s32[1,4]{1,0:T(1,128)S(1)}, s32[1,4]{1,0:T(1,128)}, u32[]{:S(2)}) copy-start(s32[1,4]{1,0:T(1,128)} %param.24) | copy-start | bytes 52
  68.9 7.8 %copy-start.1 = (bf16[4096]{0:T(1024)(128)(2,1)S(1)}, bf16[4096]{0:T(1024)(128)(2,1)}, u32[]{:S(2)}) copy-start(bf16[4096]{0:T(1024)(128)(2,1)} %param.21) | copy-start | bytes 24580
  68.9 7.8 %copy-start.5 = (bf16[1280]{0:T(1024)(128)(2,1)S(1)}, bf16[1280]{0:T(1024)(128)(2,1)}, u32[]{:S(2)}) copy-start(bf16[1280]{0:T(1024)(128)(2,1)} %param.18) | copy-start | bytes 7684
  68.9 7.8 %copy-start.6 = (bf16[1280]{0:T(1024)(128)(2,1)S(1)}, bf16[1280]{0:T(1024)(128)(2,1)}, u32[]{:S(2)}) copy-start(bf16[1280]{0:T(1024)(128)(2,1)} %param.19) | copy-start | bytes 7684
  68.9 8.1 %copy-start = (bf16[256,1280]{1,0:T(8,128)(2,1)S(1)}, bf16[256,1280]{1,0:T(8,128)(2,1)}, u32[]{:S(2)}) copy-start(bf16[256,1280]{1,0:T(8,128)(2,1)} %param.13) | copy-start | bytes 1966084
  68.9 109.3 %collective-permute-start.2 = (bf16[640,3840]{1,0:T(8,128)(2,1)}, bf16[640,3840]{1,0:T(8,128)(2,1)}, u32[]{:S(2)}, u32[]{:S(2)}) collective-permute-start(bf16[640,3840]{1,0:T(8,128)(2,1)} %maximum_select_fusion.7), channel_id=1, source_target_pairs={{0,4},{1,5},{2,6},{3,7},{4,0},{5,1},{6,2},{7,3},{8,12},{9,13},{10,... | collective-permute-start | bytes 14745608 | tf_op jit(solution)/shard_map/ppermute | solution.py:12
  74.0 60.0 %collective-permute-start.7 = (bf16[320,4096]{1,0:T(8,128)(2,1)S(1)}, bf16[320,4096]{1,0:T(8,128)(2,1)}, u32[]{:S(2)}, u32[]{:S(2)}) collective-permute-start(bf16[320,4096]{1,0:T(8,128)(2,1)S(1)} %maximum_select_fusion.16), channel_id=1, source_target_pairs={{0,2},{1,3},{2,0},{3,1},{4,6},{5,7},{6,4},{7,5},{8,10},{9,11},{10,... | collective-permute-start | bytes 7864328 | tf_op jit(solution)/shard_map/ppermute | solution.py:12
  75.6 2.4 collective-permute-start.3
  79.5 69.9 %collective-permute-start.4 = (bf16[320,1280]{1,0:T(8,128)(2,1)S(1)}, bf16[320,1280]{1,0:T(8,128)(2,1)S(1)}, u32[]{:S(2)}, u32[]{:S(2)}) collective-permute-start(bf16[320,1280]{1,0:T(8,128)(2,1)S(1)} %maximum_select_fusion.19), channel_id=1, source_target_pairs={{0,2},{1,3},{2,0},{3,1},{4,6},{5,7},{6,4},{7,5},{8,10},{9,11},{10,... | collective-permute-start | bytes 2457608 | tf_op jit(solution)/shard_map/ppermute | solution.py:12
  140.8 189.1 %collective-permute-start.8 = (bf16[640,4096]{1,0:T(8,128)(2,1)}, bf16[640,4096]{1,0:T(8,128)(2,1)}, u32[]{:S(2)}, u32[]{:S(2)}) collective-permute-start(bf16[640,4096]{1,0:T(8,128)(2,1)} %maximum_select_fusion.4), channel_id=1, source_target_pairs={{0,4},{1,5},{2,6},{3,7},{4,0},{5,1},{6,2},{7,3},{8,12},{9,13},{10,... | collective-permute-start | bytes 15728648 | tf_op jit(solution)/shard_map/ppermute | solution.py:12
  151.2 173.2 %collective-permute-start.5 = (bf16[640,1280]{1,0:T(8,128)(2,1)}, bf16[640,1280]{1,0:T(8,128)(2,1)}, u32[]{:S(2)}, u32[]{:S(2)}) collective-permute-start(bf16[640,1280]{1,0:T(8,128)(2,1)} %maximum_select_fusion.18), channel_id=1, source_target_pairs={{0,4},{1,5},{2,6},{3,7},{4,0},{5,1},{6,2},{7,3},{8,12},{9,13},{10,... | collective-permute-start | bytes 4915208 | tf_op jit(solution)/shard_map/ppermute | solution.py:12
  340.2 6.0 %copy-start.2 = (bf16[4096]{0:T(1024)(128)(2,1)S(1)}, bf16[4096]{0:T(1024)(128)(2,1)}, u32[]{:S(2)}) copy-start(bf16[4096]{0:T(1024)(128)(2,1)} %param.23) | copy-start | bytes 24580
  340.2 47.1 %all-to-all-start = ((bf16[16,16,4096]{2,1,0:T(8,128)(2,1)}), bf16[16,16,4096]{2,1,0:T(8,128)(2,1)S(1)}, u32[]{:S(2)}, u32[]{:S(2)}) async-start(bf16[16,16,4096]{2,1,0:T(8,128)(2,1)} %bitcast.31), calls=%async_computation | async-start | bytes 4194304 | tf_op jit(solution)/shard_map/all_to_all | solution.py:72
where the time goes:
time: 400 us; the launch traced here: 394 us
  waiting for transfers between devices  313 us (78%)
  other arithmetic  32.9 us (8%)
  matrix products  30.2 us (8%)
  starting transfers between devices  14.2 us (4%)
    ppermute x9, waiting for transfers between devices, swapped(): return lax.ppermute(value, axis, pairs)  274 us
    all_to_all x1, waiting for transfers between devices, send_rows(): lax.all_to_all(shaped, 'req', split_axis=0, concat_axis=0, tiled=True)  39 us
    select_n x6, other arithmetic, join_pair(): jnp.where(upper, jnp.concatenate([partner, mine], axis=0), jnp.concatenat...  22.2 us
    dot_general x1, matrix products, body(): jnp.dot(picker, embedded, preferred_element_type=jnp.float32)  10.3 us
    dot_general x1, matrix products, body(): qkv_proj = jnp.dot(normed_in, whole_qkv, preferred_element_type=jnp.float32)  8.64 us
    ppermute x9, starting transfers between devices, swapped(): return lax.ppermute(value, axis, pairs)  8.21 us
  transfers between devices with their start and end apart: 10, of which 7 were waited for; matrix products, arithmetic and copies ran while one was open for 12% of the time, Pallas kernels for 0%

commit v1 on v0

v1 whole, which is shorter than its diff:
```python
import jax
import jax.numpy as jnp
from jax import lax
from jax.experimental import pallas as pl
from jax.experimental.pallas import tpu as pltpu
from jax.sharding import PartitionSpec as P

HEAD = 64
GROUP = 8
MESH = pl.DeviceIdType.MESH
F32 = jnp.float32
BF16 = jnp.bfloat16


def flipped(index, bit):
    return index + bit - 2 * bit * ((index // bit) % 2)


def norm_rows(values, gain, bias):
    mean = jnp.mean(values, axis=-1, keepdims=True)
    centered = values - mean
    variance = jnp.mean(centered * centered, axis=-1, keepdims=True)
    return centered * lax.rsqrt(variance + 1e-05) * gain + bias


def encoder_kernel(
    frames_ref, gain1_ref, bias1_ref, gain2_ref, bias2_ref, pairs_ref,
    qkv_ref, out_w_ref, proj_ref,
    normed_ref, whole_proj,
    whole_qkv, whole_out, normed_in, residual, qkv, attended, mask,
    send_sem, recv_sem, local_sem,
):
    width = frames_ref.shape[1]
    rows = frames_ref.shape[0]
    half = rows // 2
    shard = qkv_ref.shape[0]
    g = lax.axis_index("groups")
    r = lax.axis_index("req")
    lane = g % 2
    mine = r % GROUP
    core_dev = (g, flipped(r, 1))
    y_dev = (g, flipped(r, 2))
    z_dev = (g, flipped(r, 4))
    x_dev = (flipped(g, 1), r)
    own = mine
    from_y = flipped(mine, 2)
    from_z = flipped(mine, 4)
    from_yz = flipped(from_y, 4)

    barrier = pltpu.get_barrier_semaphore()
    for device in (core_dev, y_dev, z_dev, x_dev):
        pl.semaphore_signal(barrier, inc=1, device_id=device, device_id_type=MESH)
    pl.semaphore_wait(barrier, 4)

    pieces = 4
    proj_cols = proj_ref.shape[1] // pieces
    units = [(qkv_ref, whole_qkv, j * width, width) for j in range(3)]
    units.append((out_w_ref, whole_out, 0, width))
    units += [(proj_ref, whole_proj, j * proj_cols, proj_cols) for j in range(pieces)]
    count = len(units)
    tile = 16
    step = shard // (5 * tile) * tile
    direct = shard - step
    middle = shard // 2
    first = middle // tile // 2 * tile
    second = middle - first

    def view(unit, block, start, size):
        _, whole, column, columns = units[unit]
        begin = pl.multiple_of(block * shard + start, tile)
        return whole.at[pl.ds(begin, size), pl.ds(column, columns)]

    def own_view(unit, start, size):
        source, _, column, columns = units[unit]
        return source.at[pl.ds(pl.multiple_of(start, tile), size), pl.ds(column, columns)]

    def remote(unit, which, source, target, device):
        return pltpu.make_async_remote_copy(
            src_ref=source,
            dst_ref=target,
            send_sem=send_sem.at[unit, which],
            recv_sem=recv_sem.at[unit, which],
            device_id=device,
            device_id_type=MESH,
        )

    def moved(unit, which, block, start, size, device):
        span = view(unit, block, start, size)
        return remote(unit, which, span, span, device)

    def split(unit):
        return (second, first) if unit % 2 else (first, second)

    copies = []
    locals_ = []
    for u in range(count):
        via_y, via_z = split(u)
        d0 = lane * step
        m0 = lane * middle
        copies.append([
            remote(u, 0, own_view(u, d0, direct), view(u, own, d0, direct), y_dev),
            remote(u, 1, own_view(u, d0, direct), view(u, own, d0, direct), z_dev),
            remote(u, 2, own_view(u, 0, shard), view(u, own, 0, shard), core_dev),
            moved(u, 3, from_y, lane * direct, step, x_dev),
            moved(u, 4, from_y, m0 + via_y, via_z, z_dev),
            moved(u, 5, from_y, 0, shard, core_dev),
            moved(u, 6, from_z, lane * direct, step, x_dev),
            moved(u, 7, from_z, m0, via_y, y_dev),
            moved(u, 8, from_z, 0, shard, core_dev),
            moved(u, 9, from_yz, m0 + via_y, via_z, x_dev),
            moved(u, 10, from_yz, m0, via_y, x_dev),
            moved(u, 11, from_yz, 0, shard, core_dev),
        ])
        locals_.append(
            pltpu.make_async_copy(own_view(u, 0, shard), view(u, own, 0, shard), local_sem.at[u])
        )

    def begin(u):
        if u < count:
            copies[u][0].start()
            copies[u][1].start()
            copies[u][2].start()
            locals_[u].start()

    def arrive(u):
        c = copies[u]
        c[0].wait_recv()
        c[3].start()
        c[4].start()
        c[1].wait_recv()
        c[6].start()
        c[7].start()

    def relay(u):
        c = copies[u]
        c[4].wait_recv()
        c[9].start()
        c[7].wait_recv()
        c[10].start()
        c[3].wait_recv()
        c[5].start()
        c[6].wait_recv()
        c[8].start()

    def last(u):
        c = copies[u]
        c[9].wait_recv()
        c[10].wait_recv()
        c[11].start()

    def complete(u):
        c = copies[u]
        for k in (2, 5, 8, 11):
            c[k].wait_recv()
        locals_[u].wait()

    def advance(t):
        if t < count:
            arrive(t)
            begin(t + 2)
        if 0 <= t - 1 < count:
            relay(t - 1)
        if 0 <= t - 2 < count:
            last(t - 2)

    begin(0)
    begin(1)

    place = lax.broadcasted_iota(jnp.int32, (rows, rows), 0)
    column = lax.broadcasted_iota(jnp.int32, (rows, rows), 1)
    order = (column == 2 * (place % half) + place // half).astype(BF16)
    frames = jnp.dot(order, frames_ref[...], preferred_element_type=F32)
    residual[...] = frames
    normed_in[...] = norm_rows(
        frames, gain1_ref[...].astype(F32), bias1_ref[...].astype(F32)
    ).astype(BF16)
    row_window = jnp.zeros((rows, rows), jnp.int32)
    column_window = jnp.zeros((rows, rows), jnp.int32)
    end = jnp.int32(0)
    for j in range(pairs_ref.shape[1]):
        end = end + pairs_ref[0, j]
        row_window += (place % half >= end).astype(jnp.int32)
        column_window += (column % half >= end).astype(jnp.int32)
    mask[...] = jnp.where(row_window == column_window, 0.0, -1e30).astype(F32)

    block = 256

    def project(unit):
        @pl.loop(0, width // block)
        def _(i):
            cols = pl.ds(pl.multiple_of(unit * width + i * block, block), block)
            qkv[:, cols] = jnp.dot(
                normed_in[...], whole_qkv[:, cols], preferred_element_type=F32
            ).astype(BF16)

    pair = 2 * HEAD
    upper = lax.broadcasted_iota(jnp.int32, (rows, pair), 1) >= HEAD

    def softmax(scores):
        scores = scores * HEAD ** (-0.5) + mask[...]
        powers = jnp.exp(scores - jnp.max(scores, axis=1, keepdims=True))
        return (powers * (1.0 / jnp.sum(powers, axis=1, keepdims=True))).astype(BF16)

    def heads(low, high):
        @pl.loop(low, high)
        def _(i):
            at = pl.multiple_of(i * pair, pair)
            queries = qkv[:, pl.ds(at, pair)]
            keys = qkv[:, pl.ds(pl.multiple_of(width + at, pair), pair)]
            values = qkv[:, pl.ds(pl.multiple_of(2 * width + at, pair), pair)]
            results = []
            for part in (0, 1):
                chosen = jnp.where(upper == (part == 1), queries, jnp.zeros_like(queries))
                scores = lax.dot_general(
                    chosen, keys, (((1,), (1,)), ((), ())), preferred_element_type=F32
                )
                results.append(jnp.dot(softmax(scores), values, preferred_element_type=F32))
            attended[:, pl.ds(at, pair)] = jnp.where(upper, results[1], results[0]).astype(BF16)

    total = width // pair
    advance(0)
    advance(1)
    advance(2)
    complete(0)
    project(0)
    advance(3)
    complete(1)
    project(1)
    advance(4)
    complete(2)
    project(2)
    heads(0, total // 2)
    advance(5)
    heads(total // 2, total)
    advance(6)
    complete(3)

    @pl.loop(0, width // block)
    def _(i):
        cols = pl.ds(pl.multiple_of(i * block, block), block)
        residual[:, cols] += jnp.dot(
            attended[...], whole_out[:, cols], preferred_element_type=F32
        )

    pooled = (residual[0:half, :] + residual[half:rows, :]) * 0.5
    normed_ref[...] = norm_rows(
        pooled, gain2_ref[...].astype(F32), bias2_ref[...].astype(F32)
    ).astype(BF16)
    for t in range(7, count + 2):
        advance(t)
    for u in range(4, count):
        complete(u)
    for u in range(count):
        for k in range(12):
            copies[u][k].wait_send()


def project_kernel(
    rows_ref, valid_ref, w_ref, b_ref, text_ref, gain_ref, gain_tile_ref, out_ref, embed, squares
):
    j = pl.program_id(0)
    steps = pl.num_programs(0)
    slots = rows_ref.shape[0]
    columns = w_ref.shape[1]
    lines = text_ref.shape[0]
    product = jnp.dot(rows_ref[...], w_ref[...], preferred_element_type=F32)
    product = (product + b_ref[...].astype(F32)).astype(BF16)
    product = jnp.where(valid_ref[...] > 0, product.astype(F32), 0.0)

    @pl.when(j == 0)
    def _():
        squares[...] = jnp.zeros_like(squares)

    squares[...] += jnp.sum(product * product, axis=1, keepdims=True)
    embed[:, pl.ds(pl.multiple_of(j * columns, columns), columns)] = (
        product * gain_tile_ref[...].astype(F32)
    )
    text = text_ref[...].astype(F32)
    mean = jnp.mean(text * text, axis=1, keepdims=True)
    out_ref[pl.ds(pl.multiple_of(slots + j * lines, lines), lines), :] = (
        text * lax.rsqrt(mean + 1e-06) * gain_ref[...].astype(F32)
    ).astype(BF16)

    @pl.when(j == steps - 1)
    def _():
        scale = lax.rsqrt(squares[...] / embed.shape[1] + 1e-06)
        out_ref[0:slots, :] = (embed[...] * scale).astype(BF16)


def body(
    frames, ln1_gain, ln1_bias, w_qkv, w_out, ln2_gain, ln2_bias, w_proj, b_proj,
    text_embed, rms_gain, window_pairs, row_route,
):
    rows, width = frames.shape
    devices = lax.axis_size("req")
    my_index = lax.axis_index("req")
    pooled_rows = rows // 2
    capacity = 2 * pooled_rows // devices
    slots = devices * capacity
    out_width = w_proj.shape[1]
    full = GROUP * w_qkv.shape[0]
    vmem = pl.BlockSpec(memory_space=pltpu.VMEM)
    hbm = pl.BlockSpec(memory_space=pl.ANY)
    units = 8
    normed, whole_proj = pl.pallas_call(
        encoder_kernel,
        out_shape=(
            jax.ShapeDtypeStruct((pooled_rows, width), BF16),
            jax.ShapeDtypeStruct((full, out_width), BF16),
        ),
        in_specs=[vmem] * 5 + [pl.BlockSpec(memory_space=pltpu.SMEM)] + [hbm] * 3,
        out_specs=(vmem, hbm),
        scratch_shapes=[
            pltpu.VMEM((full, 3 * width), BF16),
            pltpu.VMEM((full, width), BF16),
            pltpu.VMEM((rows, width), BF16),
            pltpu.VMEM((rows, width), F32),
            pltpu.VMEM((rows, 3 * width), BF16),
            pltpu.VMEM((rows, width), BF16),
            pltpu.VMEM((rows, rows), F32),
            pltpu.SemaphoreType.DMA((units, 12)),
            pltpu.SemaphoreType.DMA((units, 12)),
            pltpu.SemaphoreType.DMA((units,)),
        ],
        compiler_params=pltpu.CompilerParams(
            collective_id=0, has_side_effects=True, vmem_limit_bytes=50 * 2**20
        ),
        name="encoder",
    )(
        frames, ln1_gain[None], ln1_bias[None], ln2_gain[None], ln2_bias[None], window_pairs,
        w_qkv, w_out, w_proj,
    )
    route_table = row_route[:, 0].reshape(devices, pooled_rows)
    own_dest = lax.dynamic_index_in_dim(route_table, my_index, 0, keepdims=False)
    one_hot = (own_dest[:, None] == jnp.arange(devices, dtype=jnp.int32)[None, :]).astype(jnp.int32)
    slot_index = jnp.sum((jnp.cumsum(one_hot, axis=0) - one_hot) * one_hot, axis=1)
    target = own_dest * capacity + slot_index
    picker = (jnp.arange(slots, dtype=jnp.int32)[:, None] == target[None, :]).astype(BF16)
    arriving = jnp.sum((route_table == my_index).astype(jnp.int32), axis=1)
    valid = jnp.arange(capacity, dtype=jnp.int32)[None, :] < arriving[:, None]
    valid = valid.astype(F32).reshape(slots, 1)
    buffer = jnp.dot(picker, normed, preferred_element_type=F32).astype(BF16)
    arrived = lax.all_to_all(
        buffer.reshape(devices, capacity, width), "req", split_axis=0, concat_axis=0, tiled=True
    ).reshape(slots, width)
    steps = 8
    columns = out_width // steps
    text_rows = text_embed.shape[0]
    return pl.pallas_call(
        project_kernel,
        grid=(steps,),
        out_shape=jax.ShapeDtypeStruct((slots + text_rows, out_width), BF16),
        in_specs=[
            pl.BlockSpec((slots, width), lambda j: (0, 0)),
            pl.BlockSpec((slots, 1), lambda j: (0, 0)),
            pl.BlockSpec((full, columns), lambda j: (0, j)),
            pl.BlockSpec((1, columns), lambda j: (0, j)),
            pl.BlockSpec((text_rows // steps, out_width), lambda j: (j, 0)),
            pl.BlockSpec((1, out_width), lambda j: (0, 0)),
            pl.BlockSpec((1, columns), lambda j: (0, j)),
        ],
        out_specs=pl.BlockSpec((slots + text_rows, out_width), lambda j: (0, 0)),
        scratch_shapes=[pltpu.VMEM((slots, out_width), F32), pltpu.VMEM((slots, 1), F32)],
        compiler_params=pltpu.CompilerParams(vmem_limit_bytes=40 * 2**20),
        name="projector",
    )(arrived, valid, whole_proj, b_proj[None], text_embed, rms_gain[None], rms_gain[None])


def solution(mesh):
    in_specs = (
        P(("groups", "req"), None),
        P(),
        P(),
        P("req", None),
        P("req", None),
        P(),
        P(),
        P("req", None),
        P(),
        P(("groups", "req"), None),
        P(),
        P(("groups", "req"), None),
        P("groups", None),
    )
    out_specs = P(("groups", "req"), None)
    return jax.shard_map(body, mesh=mesh, in_specs=in_specs, out_specs=out_specs, check_vma=False)
```

time: 400 us -> 131 us (0.33); the launches traced: 394 us -> 131 us
  waiting for transfers between devices: 313 us -> 16.2 us
  Pallas kernels: 0 us -> 94.1 us
  other arithmetic: 32.9 us -> 1.32 us
  matrix products: 30.2 us -> 1.16 us
  local copies, waits for them, and re-layouts: 2.82 us -> 12.9 us
  starting transfers between devices: 14.2 us -> 5 us
    ppermute x9 -> x0, waiting for transfers between devices: 274 us -> none  [swapped(): return lax.ppermute(value, axis, pairs)]
    pallas_call x0 -> x2, Pallas kernels: none -> 94.1 us  [the longest x1 85.1 us: body(): pl.pallas_call(encoder_kernel, out_shape=(jax.ShapeDtypeStruct((pooled_ro...]
    dot_general x4 -> x1, matrix products: 26 us -> 1.16 us  [body(): buffer = jnp.dot(picker, normed, preferred_element_type=F32).astype(BF16)]
    all_to_all x1, waiting for transfers between devices: 39 us -> 16.2 us  [body(): lax.all_to_all(buffer.reshape(devices, capacity, width), 'req', split_axi...]
    select_n x6 -> x0, other arithmetic: 22.2 us -> none  [join_pair(): jnp.where(upper, jnp.concatenate([partner, mine], axis=0), jnp.concatenat...]
    unnamed x16 -> x20, local copies, waits for them, and re-layouts: 0.04 us -> 9.34 us
    ppermute x9 -> x0, starting transfers between devices: 8.21 us -> none  [swapped(): return lax.ppermute(value, axis, pairs)]
    sub x1 -> x0, matrix products: 4.21 us -> none  [attend(): expo_scores = jnp.exp(scores - top_score)]
  transfers between devices with their start and end apart: 10 -> 1, of which waited for: 7 -> 1; matrix products, arithmetic and copies ran while one was open for 12% -> 0% of each run, Pallas kernels for 0% -> 0%
where the time goes in v1:
time: 131 us
  Pallas kernels  94.1 us (72%)
  waiting for transfers between devices  16.2 us (12%)
  local copies, waits for them, and re-layouts  12.9 us (10%)
  starting transfers between devices  5 us (4%)
  other arithmetic  1.32 us (1%)
    pallas_call x1, Pallas kernels, body(): pl.pallas_call(encoder_kernel, out_shape=(jax.ShapeDtypeStruct((pooled_ro...  85.1 us
    all_to_all x1, waiting for transfers between devices, body(): lax.all_to_all(buffer.reshape(devices, capacity, width), 'req', split_axi...  16.2 us
    unnamed x20, local copies, waits for them, and re-layouts  9.34 us
    pallas_call x1, Pallas kernels, body(): pl.pallas_call(project_kernel, grid=(steps,), out_shape=jax.ShapeDtypeStr...  9.01 us
    all_to_all x1, starting transfers between devices, body(): lax.all_to_all(buffer.reshape(devices, capacity, width), 'req', split_axi...  5 us
  transfers between devices with their start and end apart: 1, of which 1 were waited for; matrix products, arithmetic and copies ran while one was open for 0% of the time, Pallas kernels for 0%

profile of v1, /device:TPU:0, one launch (start us, length us, event | category | flops | bytes accessed | tf_op | source)
XLA Modules:
  0.0 130.8 jit_solution(16831672756945278553)
XLA Ops:
  0.0 0.7 broadcast_in_dim.12.gain1_ref
  0.7 0.7 broadcast_in_dim.26.bias1_ref
  1.4 0.7 broadcast_in_dim.27.gain2_ref
  2.1 0.7 broadcast_in_dim.28.bias2_ref
  2.8 0.7 fusion.4
  3.5 0.1 fusion.1
  3.5 0.2 reduce_window_sum.11
  3.7 0.2 select_reduce_fusion
  3.9 0.7 fusion.3
  4.6 1.3 %copy-done.2 = bf16[160,4096]{1,0:T(8,128)(2,1)S(1)} copy-done((bf16[160,4096]{1,0:T(8,128)(2,1)S(1)}, bf16[160,4096]{1,0:T(8,128)(2,1)}, u32[]{:S(2)}) %copy-start.2) | copy-done | bytes 1310744
  5.9 1.3 copy-done.3
  7.2 1.1 copy-done.4
  8.3 1.0 copy-done.5
  9.3 0.7 copy-done.6
  10.0 85.1 %encoder.1 = (bf16[128,1280]{1,0:T(8,128)(2,1)S(1)}, bf16[1280,4096]{1,0:T(8,128)(2,1)}) custom-call(bf16[256,1280]{1,0:T(8,128)(2,1)S(1)} %copy-done.4, bf16[1,1280]{1,0:T(2,128)(2,1)S(1)} %broadcast_in_dim.12.gain1_ref, bf16[1,1280]{1,0:T(2,128)(2,1)S(1)} %broadcast_in_dim.26.bias1_ref, bf16[1,1280]{1,0:T(2,128)(2,1)S(1)} %broadcast_in_dim.27.gain2_ref, ...), custom_call_target="tpu_custom_call" | custom-call | tf_op jit(solution)/shard_map/encoder/pallas_call | solution.py:305
  95.0 0.0 copy-start.1
  95.0 1.2 convolution_convert_fusion
  96.2 5.0 %all-to-all-start = ((bf16[16,16,1280]{2,1,0:T(8,128)(2,1)}), bf16[16,16,1280]{2,1,0:T(8,128)(2,1)S(1)}, u32[]{:S(2)}, u32[]{:S(2)}) async-start(bf16[16,16,1280]{2,1,0:T(8,128)(2,1)} %bitcast.4), calls=%async_computation | async-start | bytes 1310720 | tf_op jit(solution)/shard_map/all_to_all | solution.py:343
  101.3 0.1 convert_reduce_fusion
  101.4 0.1 fusion.2
  101.5 0.1 reshape.41.valid_ref
  101.6 16.2 %all-to-all-done = bf16[16,16,1280]{2,1,0:T(8,128)(2,1)S(1)} async-done(((bf16[16,16,1280]{2,1,0:T(8,128)(2,1)}), bf16[16,16,1280]{2,1,0:T(8,128)(2,1)S(1)}, u32[]{:S(2)}, u32[]{:S(2)}) %all-to-all-start) | async-done | bytes 655392 | tf_op jit(solution)/shard_map/all_to_all | solution.py:343
  117.8 4.0 %copy-done = bf16[1280,4096]{1,0:T(8,128)(2,1)S(1)} copy-done((bf16[1280,4096]{1,0:T(8,128)(2,1)S(1)}, bf16[1280,4096]{1,0:T(8,128)(2,1)}, u32[]{:S(2)}) %copy-start) | copy-done | bytes 10485784
  121.8 9.0 %projector.1 = bf16[512,4096]{1,0:T(8,128)(2,1)} custom-call(bf16[256,1280]{1,0:T(8,128)(2,1)S(1)} %bitcast.12, f32[256,1]{1,0:T(8,128)S(1)} %reshape.41.valid_ref, bf16[1280,4096]{1,0:T(8,128)(2,1)S(1)} %copy-done, bf16[1,4096]{1,0:T(2,128)(2,1)S(1)} %broadcast_in_dim.29.b_ref, bf16[256,4096]{1,0:T(8,128)(2,1)S(1)} %copy-done.1, ...), custom_call_target="tpu_custom_call" | custom-call | tf_op jit(solution)/shard_map/projector/pallas_call | solution.py:349
  (15 shorter events, 0.0 us)
Async XLA Ops:
  4.6 1.3 %copy-start.2 = (bf16[160,4096]{1,0:T(8,128)(2,1)S(1)}, bf16[160,4096]{1,0:T(8,128)(2,1)}, u32[]{:S(2)}) copy-start(bf16[160,4096]{1,0:T(8,128)(2,1)} %proj_ref.1) | copy-start | bytes 3932164
  5.9 1.3 copy-start.3
  7.2 1.1 copy-start.4
  8.3 1.0 copy-start.5
  9.3 0.7 copy-start.6
  10.0 91.3 %copy-start.8 = (bf16[4096]{0:T(1024)(128)(2,1)S(1)}, bf16[4096]{0:T(1024)(128)(2,1)}, u32[]{:S(2)}) copy-start(bf16[4096]{0:T(1024)(128)(2,1)} %param.21) | copy-start | bytes 24580
  10.0 91.3 %copy-start.9 = (bf16[4096]{0:T(1024)(128)(2,1)S(1)}, bf16[4096]{0:T(1024)(128)(2,1)}, u32[]{:S(2)}) copy-start(bf16[4096]{0:T(1024)(128)(2,1)} %param.23) | copy-start | bytes 24580
  10.0 91.3 %copy-start.7 = (s32[2048,1]{0,1:T(1,128)S(1)}, s32[2048,1]{0,1:T(1,128)}, u32[]{:S(2)}) copy-start(s32[2048,1]{0,1:T(1,128)} %param.25) | copy-start | bytes 24580
  95.0 22.8 %copy-start.1 = (bf16[256,4096]{1,0:T(8,128)(2,1)S(1)}, bf16[256,4096]{1,0:T(8,128)(2,1)}, u32[]{:S(2)}) copy-start(bf16[256,4096]{1,0:T(8,128)(2,1)} %text_ref.1) | copy-start | bytes 6291460
  96.2 21.6 %all-to-all-start = ((bf16[16,16,1280]{2,1,0:T(8,128)(2,1)}), bf16[16,16,1280]{2,1,0:T(8,128)(2,1)S(1)}, u32[]{:S(2)}, u32[]{:S(2)}) async-start(bf16[16,16,1280]{2,1,0:T(8,128)(2,1)} %bitcast.4), calls=%async_computation | async-start | bytes 1310720 | tf_op jit(solution)/shard_map/all_to_all | solution.py:343
  117.8 4.0 %copy-start = (bf16[1280,4096]{1,0:T(8,128)(2,1)S(1)}, bf16[1280,4096]{1,0:T(8,128)(2,1)}, u32[]{:S(2)}) copy-start(bf16[1280,4096]{1,0:T(8,128)(2,1)} %get-tuple-element.8.w_ref) | copy-start | bytes 31457284

commit v2 on v1

--- a/solution.py
+++ b/solution.py
@@ -24,11 +24,12 @@
 
 
 def encoder_kernel(
-    frames_ref, gain1_ref, bias1_ref, gain2_ref, bias2_ref, pairs_ref,
+    frames_hbm, gain1_hbm, bias1_hbm, gain2_hbm, bias2_hbm, b_proj_hbm, pairs_hbm, route_ref,
     qkv_ref, out_w_ref, proj_ref,
-    normed_ref, whole_proj,
-    whole_qkv, whole_out, normed_in, residual, qkv, attended, mask,
-    send_sem, recv_sem, local_sem,
+    embed_ref,
+    whole_qkv, whole_out, whole_proj, frames_ref, gain1_ref, bias1_ref, gain2_ref, bias2_ref,
+    b_proj_ref, b_row, pairs_ref, normed_in, residual, qkv, attended, mask, buffer, arrived, packed,
+    send_sem, recv_sem, local_sem, load_sem, rows_send, rows_recv,
 ):
     width = frames_ref.shape[1]
     rows = frames_ref.shape[0]
@@ -48,9 +49,26 @@
     from_yz = flipped(from_y, 4)
 
     barrier = pltpu.get_barrier_semaphore()
-    for device in (core_dev, y_dev, z_dev, x_dev):
-        pl.semaphore_signal(barrier, inc=1, device_id=device, device_id_type=MESH)
-    pl.semaphore_wait(barrier, 4)
+    devices = route_ref.shape[0]
+
+    @pl.loop(1, devices)
+    def _(i):
+        pl.semaphore_signal(
+            barrier, inc=1, device_id=(g, (r + i) % devices), device_id_type=MESH
+        )
+
+    pl.semaphore_signal(barrier, inc=1, device_id=x_dev, device_id_type=MESH)
+    loads = [
+        pltpu.make_async_copy(source, target, load_sem.at[k])
+        for k, (source, target) in enumerate([
+            (frames_hbm, frames_ref), (gain1_hbm, gain1_ref), (bias1_hbm, bias1_ref),
+            (gain2_hbm, gain2_ref), (bias2_hbm, bias2_ref), (b_proj_hbm, b_proj_ref),
+            (pairs_hbm, pairs_ref),
+        ])
+    ]
+    for load in loads:
+        load.start()
+    pl.semaphore_wait(barrier, devices)
 
     pieces = 4
     proj_cols = proj_ref.shape[1] // pieces
@@ -165,14 +183,20 @@
 
     begin(0)
     begin(1)
-
+    for load in loads:
+        load.wait()
+
+    def row_of(ref):
+        return ref[...].reshape(1, ref.shape[0]).astype(F32)
+
+    b_row[...] = row_of(b_proj_ref)
     place = lax.broadcasted_iota(jnp.int32, (rows, rows), 0)
     column = lax.broadcasted_iota(jnp.int32, (rows, rows), 1)
     order = (column == 2 * (place % half) + place // half).astype(BF16)
     frames = jnp.dot(order, frames_ref[...], preferred_element_type=F32)
     residual[...] = frames
     normed_in[...] = norm_rows(
-        frames, gain1_ref[...].astype(F32), bias1_ref[...].astype(F32)
+        frames, row_of(gain1_ref), row_of(bias1_ref)
     ).astype(BF16)
     row_window = jnp.zeros((rows, rows), jnp.int32)
     column_window = jnp.zeros((rows, rows), jnp.int32)
@@ -243,48 +267,106 @@
         )
 
     pooled = (residual[0:half, :] + residual[half:rows, :]) * 0.5
-    normed_ref[...] = norm_rows(
-        pooled, gain2_ref[...].astype(F32), bias2_ref[...].astype(F32)
-    ).astype(BF16)
-    for t in range(7, count + 2):
-        advance(t)
-    for u in range(4, count):
-        complete(u)
+    normed = norm_rows(pooled, row_of(gain2_ref), row_of(bias2_ref)).astype(BF16)
+    capacity = 2 * half // devices
+    stride = buffer.shape[0] // devices
+    across = lax.broadcasted_iota(jnp.int32, (half, half), 1)
+    down = lax.broadcasted_iota(jnp.int32, (half, half), 0)
+    dest = route_ref[pl.ds(r, 1), :].astype(F32)
+    dest_down = jnp.sum(jnp.where(across == down, dest, 0.0), axis=1, keepdims=True)
+    earlier = jnp.where((dest_down == dest) & (down < across), 1.0, 0.0)
+    target = dest * stride + jnp.sum(earlier, axis=0, keepdims=True)
+    slot = lax.broadcasted_iota(jnp.int32, (buffer.shape[0], half), 0)
+    picker = (slot == target.astype(jnp.int32)).astype(BF16)
+    buffer[...] = jnp.dot(picker, normed, preferred_element_type=F32).astype(BF16)
+
+    def exchange(i):
+        to = (r + i) % devices
+        return pltpu.make_async_remote_copy(
+            src_ref=buffer.at[pl.ds(pl.multiple_of(to * stride, tile), stride), :],
+            dst_ref=arrived.at[pl.ds(pl.multiple_of(r * stride, tile), stride), :],
+            send_sem=rows_send.at[i],
+            recv_sem=rows_recv.at[i],
+            device_id=(g, to),
+            device_id_type=MESH,
+        )
+
+    @pl.loop(1, devices)
+    def _(i):
+        exchange(i).start()
+
+    mine_rows = pl.ds(pl.multiple_of(r * stride, tile), stride)
+    stay = pltpu.make_async_copy(
+        buffer.at[mine_rows, :], arrived.at[mine_rows, :], local_sem.at[count]
+    )
+    stay.start()
+    advance(7)
+    advance(8)
+
+    @pl.loop(1, devices)
+    def _(i):
+        exchange(i).wait_recv()
+
+    stay.wait()
+    slots = devices * capacity
+    if capacity == stride:
+        packed[...] = arrived[...]
+    else:
+        row = lax.broadcasted_iota(jnp.int32, (slots, devices * stride), 0)
+        wide = lax.broadcasted_iota(jnp.int32, (slots, devices * stride), 1)
+        keep = (wide == row // capacity * stride + row % capacity).astype(BF16)
+        packed[...] = jnp.dot(keep, arrived[...], preferred_element_type=F32).astype(BF16)
+    sender = lax.broadcasted_iota(jnp.int32, (slots, devices), 1)
+    place = lax.broadcasted_iota(jnp.int32, (slots, devices), 0)
+    spread = (place // capacity == sender).astype(BF16)
+    named = jnp.where(route_ref[...] == r, 1.0, 0.0).astype(BF16)
+    filled = jnp.sum(
+        jnp.dot(spread, named, preferred_element_type=F32), axis=1, keepdims=True
+    )
+    order = lax.broadcasted_iota(jnp.int32, (slots, 1), 0) % capacity
+    valid = order.astype(F32) < filled
+
+    def embed(piece):
+        @pl.loop(0, proj_cols // block)
+        def _(i):
+            cols = pl.ds(pl.multiple_of(piece * proj_cols + i * block, block), block)
+            product = jnp.dot(packed[...], whole_proj[:, cols], preferred_element_type=F32)
+            embed_ref[:, cols] = jnp.where(valid, product + b_row[:, cols], 0.0).astype(BF16)
+
+    complete(4)
+    embed(0)
+    complete(5)
+    embed(1)
+    advance(9)
+    complete(6)
+    embed(2)
+    complete(7)
+    embed(3)
     for u in range(count):
         for k in range(12):
             copies[u][k].wait_send()
 
-
-def project_kernel(
-    rows_ref, valid_ref, w_ref, b_ref, text_ref, gain_ref, gain_tile_ref, out_ref, embed, squares
-):
+    @pl.loop(1, devices)
+    def _(i):
+        exchange(i).wait_send()
+
+
+def rms_kernel(audio_ref, text_ref, gain_ref, out_ref):
     j = pl.program_id(0)
-    steps = pl.num_programs(0)
-    slots = rows_ref.shape[0]
-    columns = w_ref.shape[1]
-    lines = text_ref.shape[0]
-    product = jnp.dot(rows_ref[...], w_ref[...], preferred_element_type=F32)
-    product = (product + b_ref[...].astype(F32)).astype(BF16)
-    product = jnp.where(valid_ref[...] > 0, product.astype(F32), 0.0)
-
-    @pl.when(j == 0)
+    steps = pl.num_programs(0) // 2
+
+    def write(ref):
+        values = ref[...].astype(F32)
+        mean = jnp.mean(values * values, axis=1, keepdims=True)
+        out_ref[...] = (values * lax.rsqrt(mean + 1e-06) * gain_ref[...].astype(F32)).astype(BF16)
+
+    @pl.when(j < steps)
     def _():
-        squares[...] = jnp.zeros_like(squares)
-
-    squares[...] += jnp.sum(product * product, axis=1, keepdims=True)
-    embed[:, pl.ds(pl.multiple_of(j * columns, columns), columns)] = (
-        product * gain_tile_ref[...].astype(F32)
-    )
-    text = text_ref[...].astype(F32)
-    mean = jnp.mean(text * text, axis=1, keepdims=True)
-    out_ref[pl.ds(pl.multiple_of(slots + j * lines, lines), lines), :] = (
-        text * lax.rsqrt(mean + 1e-06) * gain_ref[...].astype(F32)
-    ).astype(BF16)
-
-    @pl.when(j == steps - 1)
+        write(audio_ref)
+
+    @pl.when(j >= steps)
     def _():
-        scale = lax.rsqrt(squares[...] / embed.shape[1] + 1e-06)
-        out_ref[0:slots, :] = (embed[...] * scale).astype(BF16)
+        write(text_ref)
 
 
 def body(
@@ -293,7 +375,6 @@
 ):
     rows, width = frames.shape
     devices = lax.axis_size("req")
-    my_index = lax.axis_index("req")
     pooled_rows = rows // 2
     capacity = 2 * pooled_rows // devices
     slots = devices * capacity
@@ -302,68 +383,64 @@
     vmem = pl.BlockSpec(memory_space=pltpu.VMEM)
     hbm = pl.BlockSpec(memory_space=pl.ANY)
     units = 8
-    normed, whole_proj = pl.pallas_call(
+    stride = max(capacity, 16)
+    route_table = row_route.reshape(devices, pooled_rows)
+    embed = pl.pallas_call(
         encoder_kernel,
-        out_shape=(
-            jax.ShapeDtypeStruct((pooled_rows, width), BF16),
-            jax.ShapeDtypeStruct((full, out_width), BF16),
-        ),
-        in_specs=[vmem] * 5 + [pl.BlockSpec(memory_space=pltpu.SMEM)] + [hbm] * 3,
-        out_specs=(vmem, hbm),
+        out_shape=jax.ShapeDtypeStruct((slots, out_width), BF16),
+        in_specs=[hbm] * 7 + [vmem] + [hbm] * 3,
+        out_specs=vmem,
         scratch_shapes=[
             pltpu.VMEM((full, 3 * width), BF16),
             pltpu.VMEM((full, width), BF16),
+            pltpu.VMEM((full, out_width), BF16),
+            pltpu.VMEM((rows, width), BF16),
+            pltpu.VMEM((width,), BF16),
+            pltpu.VMEM((width,), BF16),
+            pltpu.VMEM((width,), BF16),
+            pltpu.VMEM((width,), BF16),
+            pltpu.VMEM((out_width,), BF16),
+            pltpu.VMEM((1, out_width), F32),
+            pltpu.SMEM(window_pairs.shape, jnp.int32),
             pltpu.VMEM((rows, width), BF16),
             pltpu.VMEM((rows, width), F32),
             pltpu.VMEM((rows, 3 * width), BF16),
             pltpu.VMEM((rows, width), BF16),
             pltpu.VMEM((rows, rows), F32),
+            pltpu.VMEM((devices * stride, width), BF16),
+            pltpu.VMEM((devices * stride, width), BF16),
+            pltpu.VMEM((slots, width), BF16),
             pltpu.SemaphoreType.DMA((units, 12)),
             pltpu.SemaphoreType.DMA((units, 12)),
-            pltpu.SemaphoreType.DMA((units,)),
+            pltpu.SemaphoreType.DMA((units + 1,)),
+            pltpu.SemaphoreType.DMA((7,)),
+            pltpu.SemaphoreType.DMA((devices,)),
+            pltpu.SemaphoreType.DMA((devices,)),
         ],
         compiler_params=pltpu.CompilerParams(
-            collective_id=0, has_side_effects=True, vmem_limit_bytes=50 * 2**20
+            collective_id=0, has_side_effects=True, vmem_limit_bytes=58 * 2**20
         ),
         name="encoder",
     )(
-        frames, ln1_gain[None], ln1_bias[None], ln2_gain[None], ln2_bias[None], window_pairs,
+        frames, ln1_gain, ln1_bias, ln2_gain, ln2_bias, b_proj, window_pairs, route_table,
         w_qkv, w_out, w_proj,
     )
-    route_table = row_route[:, 0].reshape(devices, pooled_rows)
-    own_dest = lax.dynamic_index_in_dim(route_table, my_index, 0, keepdims=False)
-    one_hot = (own_dest[:, None] == jnp.arange(devices, dtype=jnp.int32)[None, :]).astype(jnp.int32)
-    slot_index = jnp.sum((jnp.cumsum(one_hot, axis=0) - one_hot) * one_hot, axis=1)
-    target = own_dest * capacity + slot_index
-    picker = (jnp.arange(slots, dtype=jnp.int32)[:, None] == target[None, :]).astype(BF16)
-    arriving = jnp.sum((route_table == my_index).astype(jnp.int32), axis=1)
-    valid = jnp.arange(capacity, dtype=jnp.int32)[None, :] < arriving[:, None]
-    valid = valid.astype(F32).reshape(slots, 1)
-    buffer = jnp.dot(picker, normed, preferred_element_type=F32).astype(BF16)
-    arrived = lax.all_to_all(
-        buffer.reshape(devices, capacity, width), "req", split_axis=0, concat_axis=0, tiled=True
-    ).reshape(slots, width)
-    steps = 8
-    columns = out_width // steps
     text_rows = text_embed.shape[0]
+    steps = 4
+    audio_block = slots // steps
     return pl.pallas_call(
-        project_kernel,
-        grid=(steps,),
+        rms_kernel,
+        grid=(2 * steps,),
         out_shape=jax.ShapeDtypeStruct((slots + text_rows, out_width), BF16),
         in_specs=[
-            pl.BlockSpec((slots, width), lambda j: (0, 0)),
-            pl.BlockSpec((slots, 1), lambda j: (0, 0)),
-            pl.BlockSpec((full, columns), lambda j: (0, j)),
-            pl.BlockSpec((1, columns), lambda j: (0, j)),
-            pl.BlockSpec((text_rows // steps, out_width), lambda j: (j, 0)),
+            pl.BlockSpec((audio_block, out_width), lambda j: (jnp.minimum(j, steps - 1), 0)),
+            pl.BlockSpec((audio_block, out_width), lambda j: (jnp.maximum(j - steps, 0), 0)),
             pl.BlockSpec((1, out_width), lambda j: (0, 0)),
-            pl.BlockSpec((1, columns), lambda j: (0, j)),
         ],
-        out_specs=pl.BlockSpec((slots + text_rows, out_width), lambda j: (0, 0)),
-        scratch_shapes=[pltpu.VMEM((slots, out_width), F32), pltpu.VMEM((slots, 1), F32)],
-        compiler_params=pltpu.CompilerParams(vmem_limit_bytes=40 * 2**20),
-        name="projector",
-    )(arrived, valid, whole_proj, b_proj[None], text_embed, rms_gain[None], rms_gain[None])
+        out_specs=pl.BlockSpec((audio_block, out_width), lambda j: (j, 0)),
+        compiler_params=pltpu.CompilerParams(vmem_limit_bytes=58 * 2**20),
+        name="rms",
+    )(embed, text_embed, rms_gain[None])
 
 
 def solution(mesh):

time: 131 us -> 107 us (0.82)
  waiting for transfers between devices: 16.2 us -> 0 us
  local copies, waits for them, and re-layouts: 12.9 us -> 1.3 us
  Pallas kernels: 94.1 us -> 105 us
  starting transfers between devices: 5 us -> 0 us
  other arithmetic: 1.32 us -> 0 us
    all_to_all x1 -> x0, waiting for transfers between devices: 16.2 us -> none  [body(): lax.all_to_all(buffer.reshape(devices, capacity, width), 'req', split_axi...]
    pallas_call x2, Pallas kernels: 94.1 us -> 105 us  [the longest x1 97.4 us: body(): pl.pallas_call(encoder_kernel, out_shape=jax.ShapeDtypeStruct((slots, out...]
    unnamed x20 -> x0, local copies, waits for them, and re-layouts: 9.34 us -> none
    all_to_all x1 -> x0, starting transfers between devices: 5 us -> none  [body(): lax.all_to_all(buffer.reshape(devices, capacity, width), 'req', split_axi...]
    broadcast_in_dim x5 -> x0, local copies, waits for them, and re-layouts: 2.78 us -> none  [the longest x1 0.69 us: body(): ln1_gain[None]]
  transfers between devices with their start and end apart: 1 -> 0, of which waited for: 1 -> 0; matrix products, arithmetic and copies ran while one was open for 0% -> 0% of each run, Pallas kernels for 0% -> 0%
where the time goes in v2:
time: 107 us; the launch traced here: 106 us
  Pallas kernels  105 us (98%)
  local copies, waits for them, and re-layouts  1.3 us (1%)
    pallas_call x1, Pallas kernels, body(): pl.pallas_call(encoder_kernel, out_shape=jax.ShapeDtypeStruct((slots, out...  97.4 us
    pallas_call x1, Pallas kernels, body(): pl.pallas_call(rms_kernel, grid=(2 * steps,), out_shape=jax.ShapeDtypeStr...  7.6 us

profile of v2, /device:TPU:0, one launch (start us, length us, event | category | flops | bytes accessed | tf_op | source)
XLA Modules:
  0.0 106.3 jit_solution(10836525225729053221)
XLA Ops:
  0.0 1.3 %broadcast_in_dim.3.gain_ref = bf16[1,4096]{1,0:T(2,128)(2,1)} reshape(bf16[4096]{0:T(1024)(128)(2,1)} %param.23) | data formatting | bytes 16384 | tf_op jit(solution)/shard_map/broadcast_in_dim | solution.py:443
  1.3 97.4 %encoder.1.audio_ref = bf16[256,4096]{1,0:T(8,128)(2,1)} custom-call(bf16[256,1280]{1,0:T(8,128)(2,1)} %frames_hbm.1, bf16[1280]{0:T(1024)(128)(2,1)} %gain1_hbm.1, bf16[1280]{0:T(1024)(128)(2,1)} %bias1_hbm.1, bf16[1280]{0:T(1024)(128)(2,1)} %gain2_hbm.1, bf16[1280]{0:T(1024)(128)(2,1)} %bias2_hbm.1, bf16[4096]{0:T(1024)(128)(2,1)} %b_proj_hbm.1, ...), custom_call_target="tpu_custom_call" | custom-call | tf_op jit(solution)/shard_map/encoder/pallas_call | solution.py:388
  98.7 7.6 %rms.1 = bf16[512,4096]{1,0:T(8,128)(2,1)} custom-call(bf16[256,4096]{1,0:T(8,128)(2,1)} %encoder.1.audio_ref, bf16[256,4096]{1,0:T(8,128)(2,1)} %text_ref.1, bf16[1,4096]{1,0:T(2,128)(2,1)} %broadcast_in_dim.3.gain_ref), custom_call_target="tpu_custom_call" | custom-call | tf_op jit(solution)/shard_map/rms/pallas_call | solution.py:431

commit v3 on v2

--- a/solution.py
+++ b/solution.py
@@ -357,8 +357,9 @@
 
     def write(ref):
         values = ref[...].astype(F32)
+        gain = gain_ref[...].reshape(1, gain_ref.shape[0]).astype(F32)
         mean = jnp.mean(values * values, axis=1, keepdims=True)
-        out_ref[...] = (values * lax.rsqrt(mean + 1e-06) * gain_ref[...].astype(F32)).astype(BF16)
+        out_ref[...] = (values * lax.rsqrt(mean + 1e-06) * gain).astype(BF16)
 
     @pl.when(j < steps)
     def _():
@@ -426,7 +427,7 @@
         w_qkv, w_out, w_proj,
     )
     text_rows = text_embed.shape[0]
-    steps = 4
+    steps = 2
     audio_block = slots // steps
     return pl.pallas_call(
         rms_kernel,
@@ -435,12 +436,12 @@
         in_specs=[
             pl.BlockSpec((audio_block, out_width), lambda j: (jnp.minimum(j, steps - 1), 0)),
             pl.BlockSpec((audio_block, out_width), lambda j: (jnp.maximum(j - steps, 0), 0)),
-            pl.BlockSpec((1, out_width), lambda j: (0, 0)),
+            pl.BlockSpec((out_width,), lambda j: (0,)),
         ],
         out_specs=pl.BlockSpec((audio_block, out_width), lambda j: (j, 0)),
         compiler_params=pltpu.CompilerParams(vmem_limit_bytes=58 * 2**20),
         name="rms",
-    )(embed, text_embed, rms_gain[None])
+    )(embed, text_embed, rms_gain)
 
 
 def solution(mesh):

time: 107 us -> 104 us (0.972)
  Pallas kernels: 105 us -> 103 us
  local copies, waits for them, and re-layouts: 1.3 us -> 0 us
    pallas_call x1, Pallas kernels: 7.6 us -> 5.97 us  [body(): pl.pallas_call(rms_kernel, grid=(2 * steps,), out_shape=jax.ShapeDtypeStr...]
    broadcast_in_dim x1 -> x0, local copies, waits for them, and re-layouts: 1.3 us -> none  [body(): rms_gain[None]]
where the time goes in v3:
time: 104 us; the launch traced here: 103 us
  Pallas kernels  103 us (99%)
    pallas_call x1, Pallas kernels, body(): pl.pallas_call(encoder_kernel, out_shape=jax.ShapeDtypeStruct((slots, out...  97.4 us
    pallas_call x1, Pallas kernels, body(): pl.pallas_call(rms_kernel, grid=(2 * steps,), out_shape=jax.ShapeDtypeStr...  5.97 us

profile of v3, /device:TPU:0, one launch (start us, length us, event | category | flops | bytes accessed | tf_op | source)
XLA Modules:
  0.0 103.4 jit_solution(13162496890921948559)
XLA Ops:
  0.0 97.4 %encoder.1.audio_ref = bf16[256,4096]{1,0:T(8,128)(2,1)} custom-call(bf16[256,1280]{1,0:T(8,128)(2,1)} %frames_hbm.1, bf16[1280]{0:T(1024)(128)(2,1)} %gain1_hbm.1, bf16[1280]{0:T(1024)(128)(2,1)} %bias1_hbm.1, bf16[1280]{0:T(1024)(128)(2,1)} %gain2_hbm.1, bf16[1280]{0:T(1024)(128)(2,1)} %bias2_hbm.1, bf16[4096]{0:T(1024)(128)(2,1)} %b_proj_hbm.1, ...), custom_call_target="tpu_custom_call" | custom-call | tf_op jit(solution)/shard_map/encoder/pallas_call | solution.py:389
  97.4 6.0 %rms.1 = bf16[512,4096]{1,0:T(8,128)(2,1)} custom-call(bf16[256,4096]{1,0:T(8,128)(2,1)} %encoder.1.audio_ref, bf16[256,4096]{1,0:T(8,128)(2,1)} %text_ref.1, bf16[4096]{0:T(1024)(128)(2,1)} %gain_ref.1), custom_call_target="tpu_custom_call" | custom-call | tf_op jit(solution)/shard_map/rms/pallas_call | solution.py:432

commit v4 on v3

--- a/solution.py
+++ b/solution.py
@@ -173,13 +173,13 @@
         locals_[u].wait()
 
     def advance(t):
+        if 0 <= t - 2 < count:
+            last(t - 2)
+        if 0 <= t - 1 < count:
+            relay(t - 1)
         if t < count:
             arrive(t)
             begin(t + 2)
-        if 0 <= t - 1 < count:
-            relay(t - 1)
-        if 0 <= t - 2 < count:
-            last(t - 2)
 
     begin(0)
     begin(1)

time: 104 us -> 104 us (level)
  no operation moved by 1% of the time
where the time goes in v4:
time: 104 us
  Pallas kernels  104 us (100%)
    pallas_call x1, Pallas kernels, body(): pl.pallas_call(encoder_kernel, out_shape=jax.ShapeDtypeStruct((slots, out...  97.6 us
    pallas_call x1, Pallas kernels, body(): pl.pallas_call(rms_kernel, grid=(2 * steps,), out_shape=jax.ShapeDtypeStr...  5.97 us

profile of v4, /device:TPU:0, one launch (start us, length us, event | category | flops | bytes accessed | tf_op | source)
XLA Modules:
  0.0 103.5 jit_solution(13724716281802974173)
XLA Ops:
  0.0 97.6 %encoder.1.audio_ref = bf16[256,4096]{1,0:T(8,128)(2,1)} custom-call(bf16[256,1280]{1,0:T(8,128)(2,1)} %frames_hbm.1, bf16[1280]{0:T(1024)(128)(2,1)} %gain1_hbm.1, bf16[1280]{0:T(1024)(128)(2,1)} %bias1_hbm.1, bf16[1280]{0:T(1024)(128)(2,1)} %gain2_hbm.1, bf16[1280]{0:T(1024)(128)(2,1)} %bias2_hbm.1, bf16[4096]{0:T(1024)(128)(2,1)} %b_proj_hbm.1, ...), custom_call_target="tpu_custom_call" | custom-call | tf_op jit(solution)/shard_map/encoder/pallas_call | solution.py:389
  97.6 6.0 %rms.1 = bf16[512,4096]{1,0:T(8,128)(2,1)} custom-call(bf16[256,4096]{1,0:T(8,128)(2,1)} %encoder.1.audio_ref, bf16[256,4096]{1,0:T(8,128)(2,1)} %text_ref.1, bf16[4096]{0:T(1024)(128)(2,1)} %gain_ref.1), custom_call_target="tpu_custom_call" | custom-call | tf_op jit(solution)/shard_map/rms/pallas_call | solution.py:432
